TPU v7x, 512 devices: a whole 4x4x16 slice. The times are simulated.
512 devices in a mesh: tm: 4 (over x), height: 8 (over z_lo, core), chan: 16 (over z_hi, y).
Axes of the slice: x: 4, y: 4, z: 16 (z_hi: 4, z_lo: 4; z = z_hi * 4 + z_lo), core: 2. Of those that a mesh axis runs over, the one named last changes fastest.
Arguments:
- features: bfloat16 [384, 8, 32, 160], P('chan', 'tm', 'height'), may hold values from -400 to 400, as said below
- cotangent: bfloat16 [384, 8, 32, 160], P('chan', 'tm', 'height'), may hold values from -6 to 6
- conv_weight: bfloat16 [384, 27, 384], P('chan'), may hold values from -0.0625 to 0.0625
- norm_gain: float32 [384], replicated, may hold values from 0.5 to 1.5
- norm_bias: float32 [384], replicated, may hold values from -3 to 3
Outputs:
- input_grad: bfloat16 [384, 8, 32, 160], P('chan', 'tm', 'height')
- weight_grad: float32 [384, 27, 384], P('chan')
Inputs may be any that keep to these rules, and one draw needn't show every extreme that they name: `features`: bounded activations.
All inputs are finite; a program needn't handle non-finite values.
Results may differ from a plain program's by a relative error of at most 0.003.
Values may be sent and summed in bfloat16 or wider, within the bound.
A program may use at most 64 MiB of HBM per device.

v0:
```python
import math
import jax
import jax.numpy as jnp
from jax import lax
from jax.sharding import PartitionSpec as P


def from_behind(block, axis, distance):
    devices = range(lax.axis_size(axis))
    route = [(i - distance, i) for i in devices if i - distance in devices]
    return lax.ppermute(block, axis, route)


def with_halo(array, sides, width):
    for axis, dim in sides:
        size, length = (lax.axis_size(axis), array.shape[dim])
        up = [(i, (i + 1) % size) for i in range(size - 1)]
        down = [(j, i) for i, j in up]
        last = lax.slice_in_dim(array, length - width, length, axis=dim)
        first = lax.slice_in_dim(array, 0, width, axis=dim)
        before = lax.ppermute(last, axis, up)
        after = lax.ppermute(first, axis, down)
        array = jnp.concatenate([before, array, after], axis=dim)
    return array


def on_device(features, cotangent, conv_weight, norm_gain, norm_bias):
    chans, frames, rows, cols = features.shape
    whole_x = lax.all_gather(features, "chan", axis=0, tiled=True)
    total = whole_x.shape[0]
    flat_x = whole_x.reshape(total, -1).astype(jnp.float32)
    inv_rms = lax.rsqrt(jnp.mean(flat_x * flat_x, axis=0, keepdims=True) + 1e-06)
    normed = flat_x * inv_rms * norm_gain[:, None] + norm_bias[:, None]
    active = jax.nn.silu(normed).astype(jnp.bfloat16)
    ahead = from_behind(cotangent, "tm", -1)
    longer = jnp.concatenate([cotangent, ahead], axis=1)
    bordered = with_halo(longer, (("height", 2),), 1)
    padded = jnp.pad(bordered, ((0, 0), (0, 0), (0, 0), (1, 1)))
    taps = []
    for kt in range(3):
        for kh in range(3):
            for kw in range(3):
                taps.append(
                    padded[
                        :, 2 - kt : 2 - kt + frames, 2 - kh : 2 - kh + rows, 2 - kw : 2 - kw + cols
                    ]
                )
    stacked = jnp.stack(taps, axis=1).reshape(chans * 27, -1)
    local_sums = lax.dot_general(
        stacked, active, (((1,), (1,)), ((), ())), preferred_element_type=jnp.float32
    )
    positions = frames * lax.axis_size("tm") * rows * lax.axis_size("height") * cols
    summed = lax.psum(local_sums, ("tm", "height"))
    weight_grad = (summed / math.sqrt(positions)).reshape(chans, 27, total)
    sig = jax.nn.sigmoid(normed)
    slope = sig * (1.0 + normed * (1.0 - sig))
    offset = lax.axis_index("chan") * chans
    weight_flat = conv_weight.reshape(chans * 27, total)
    partial_value = lax.dot_general(
        weight_flat, stacked, (((0,), (0,)), ((), ())), preferred_element_type=jnp.float32
    )
    act_grad = lax.psum(partial_value, "chan")
    upstream = act_grad * slope * norm_gain[:, None]
    dots = jnp.sum(upstream * flat_x, axis=0, keepdims=True)
    back = inv_rms * upstream - flat_x * inv_rms**3 * dots / total
    own_back = lax.dynamic_slice_in_dim(back, offset, chans, 0)
    result = cotangent.reshape(chans, -1).astype(jnp.float32) + own_back
    return (result.astype(jnp.bfloat16).reshape(features.shape), weight_grad)


def solution(mesh):
    return jax.shard_map(
        on_device,
        mesh=mesh,
        in_specs=(
            P("chan", "tm", "height", None),
            P("chan", "tm", "height", None),
            P("chan", None, None),
            P(),
            P(),
        ),
        out_specs=(P("chan", "tm", "height", None), P("chan", None, None)),
        check_vma=False,
    )
```

profile of v0, /device:TPU:6, one launch (start us, length us, event | category | flops | bytes accessed | tf_op | source)
XLA Modules:
  0.0 687.3 jit_solution(8743268547803639951)
XLA Ops:
  7.2 2.7 collective-permute-start
  10.0 96.6 %all_gather.3 = bf16[384,2,4,160]{3,2,1,0:T(4,128)(2,1)S(1)} all-gather(bf16[24,2,4,160]{3,2,1,0:T(4,128)(2,1)} %param.5), channel_id=1, replica_groups=mesh['tm'=4,'height'=8,'chan'=16] {'chan'}, dimensions={0}, use_global_device_ids=true | all-gather | bytes 1044480 | tf_op jit(solution)/shard_map/all_gather | solution.py:29
  106.5 1.4 copy.18
  108.0 0.4 multiply_reduce_fusion.1
  108.6 1.9 collective-permute-start.1
  110.5 1.3 collective-permute-start.2
  111.8 1.7 multiply_convert_fusion
  113.7 0.8 fusion.10
  117.6 2.4 copy.19
  120.0 5.5 reshape.64
  125.5 3.2 fusion.39
  128.7 0.2 all-reduce.4.cloned.1.call-start
  128.9 1.1 copy.20
  130.0 1.0 reshape.65
  131.0 3.6 convolution_bitcast_fusion
  134.6 1.0 copy.17
  135.7 1.5 bitcast_convert_fusion
  137.2 261.6 %all-reduce.6.cloned.1.call-done = f32[648,384]{1,0:T(8,128)} async-done(((f32[648,384]{1,0:T(8,128)}), f32[648,384]{1,0:T(8,128)}) %all-reduce.6.cloned.1.call-update) | async-done | bytes 995344 | tf_op jit(solution)/shard_map/psum | solution.py:53
  398.7 1.3 broadcast_multiply_fusion
  400.2 1.5 copy.22
  401.7 272.7 %all-reduce.4.cloned.1.call-done = f32[384,1280]{0,1:T(8,128)} async-done(((f32[384,1280]{0,1:T(8,128)}), f32[384,1280]{0,1:T(8,128)}) %all-reduce.4.cloned.1.call-update) | async-done | bytes 1966096 | tf_op jit(solution)/shard_map/psum | solution.py:62
  674.4 3.0 multiply_reduce_fusion
  677.3 2.2 fusion.3
  679.6 0.8 copy.21
  (48 shorter events, 3.7 us)
Async XLA Ops:
  7.2 101.2 %copy-start.1 = (bf16[24,2,4,160]{3,2,1,0:T(4,128)(2,1)S(1)}, bf16[24,2,4,160]{3,2,1,0:T(4,128)(2,1)}, u32[]{:S(2)}) copy-start(bf16[24,2,4,160]{3,2,1,0:T(4,128)(2,1)} %param.6) | copy-start | bytes 184324
  7.2 104.6 %copy-start.3 = (f32[384]{0:T(512)S(1)}, f32[384]{0:T(512)}, u32[]{:S(2)}) copy-start(f32[384]{0:T(512)} %param.8) | copy-start | bytes 4612
  7.2 104.6 %copy-start.2 = (f32[384]{0:T(512)S(1)}, f32[384]{0:T(512)}, u32[]{:S(2)}) copy-start(f32[384]{0:T(512)} %param.9) | copy-start | bytes 4612
  7.2 391.6 %all-reduce.6.cloned.1.call-start = ((), (), s32[]{:S(2)}) async-start(), calls=%async_computation.1 | async-start | bytes 1990656 | tf_op jit(solution)/shard_map/psum | solution.py:53
  7.2 101.2 %collective-permute-start = (bf16[24,2,4,160]{3,2,1,0:T(4,128)(2,1)}, bf16[24,2,4,160]{3,2,1,0:T(4,128)(2,1)S(1)}, u32[]{:S(2)}, u32[]{:S(2)}) collective-permute-start(bf16[24,2,4,160]{3,2,1,0:T(4,128)(2,1)} %param.6), channel_id=1, source_target_pairs={{128,0},{256,128},{384,256},{129,1},{257,129},{385,257},{130,2},{2... | collective-permute-start | bytes 184328 | tf_op jit(solution)/shard_map/ppermute | solution.py:11
  108.6 4.9 collective-permute-start.1
  110.5 3.2 collective-permute-start.2
  128.7 545.7 %all-reduce.4.cloned.1.call-start = ((), (), s32[]{:S(2)}) async-start(), calls=%async_computation | async-start | bytes 3932160 | tf_op jit(solution)/shard_map/psum | solution.py:62
  401.7 275.6 %copy-start = (f32[24,2,4,160]{0,3,2,1:T(8,128)S(1)}, f32[24,2,4,160]{0,3,2,1:T(8,128)}, u32[]{:S(2)}) copy-start(f32[24,2,4,160]{0,3,2,1:T(8,128)} %copy.17) | copy-start | bytes 368644
Sparse Core Ops, SparseCore 0:
  128.8 269.9 all-reduce.5
  402.0 272.3 all-reduce.3
where the time goes:
time: 688 us; the launch traced here: 687 us
  waiting for transfers between devices  534 us (78%)
  blocking collectives  96.6 us (14%)
  local copies, waits for them, and re-layouts  17.4 us (3%)
  between operations  14.3 us (2%)
  other arithmetic  11.7 us (2%)
    psum x1, waiting for transfers between devices, on_device(): act_grad = lax.psum(partial_value, 'chan')  273 us
    psum x1, waiting for transfers between devices, on_device(): summed = lax.psum(local_sums, ('tm', 'height'))  262 us
    all_gather x1, blocking collectives, on_device(): whole_x = lax.all_gather(features, 'chan', axis=0, tiled=True)  96.6 us
  transfers between devices with their start and end apart: 5, of which 3 were waited for; matrix products, arithmetic and copies ran while one was open for 2% of the time, Pallas kernels for 0%

commit v1 on v0

--- a/solution.py
+++ b/solution.py
@@ -50,7 +50,7 @@
         stacked, active, (((1,), (1,)), ((), ())), preferred_element_type=jnp.float32
     )
     positions = frames * lax.axis_size("tm") * rows * lax.axis_size("height") * cols
-    summed = lax.psum(local_sums, ("tm", "height"))
+    summed = jnp.sum(lax.all_gather(local_sums, ("tm", "height")), axis=0)
     weight_grad = (summed / math.sqrt(positions)).reshape(chans, 27, total)
     sig = jax.nn.sigmoid(normed)
     slope = sig * (1.0 + normed * (1.0 - sig))

time: 688 us -> 491 us (0.71)
  waiting for transfers between devices: 534 us -> 282 us
  blocking collectives: 96.6 us -> 147 us
  other arithmetic: 11.7 us -> 18.6 us
    psum x1 -> x0, waiting for transfers between devices: 262 us -> none  [on_device(): summed = lax.psum(local_sums, ('tm', 'height'))]
    all_gather x1, blocking collectives: 96.6 us -> 147 us  [on_device(): whole_x = lax.all_gather(features, 'chan', axis=0, tiled=True)]
    reduce_sum x0 -> x1, other arithmetic: none -> 11.6 us  [on_device(): summed = jnp.sum(lax.all_gather(local_sums, ('tm', 'height')), axis=0)]
  transfers between devices with their start and end apart: 5 -> 5, of which waited for: 3 -> 3; matrix products, arithmetic and copies ran while one was open for 2% -> 3% of each run, Pallas kernels for 0% -> 0%
where the time goes in v1:
time: 491 us; the launch traced here: 489 us
  waiting for transfers between devices  282 us (57%)
  blocking collectives  147 us (30%)
  other arithmetic  18.6 us (4%)
  between operations  15.8 us (3%)
  local copies, waits for them, and re-layouts  14.4 us (3%)
  matrix products  5.97 us (1%)
  starting transfers between devices  5.41 us (1%)
    psum x1, waiting for transfers between devices, on_device(): act_grad = lax.psum(partial_value, 'chan')  278 us
    all_gather x1, blocking collectives, on_device(): whole_x = lax.all_gather(features, 'chan', axis=0, tiled=True)  147 us
    reduce_sum x1, other arithmetic, on_device(): summed = jnp.sum(lax.all_gather(local_sums, ('tm', 'height')), axis=0)  11.6 us
  transfers between devices with their start and end apart: 5, of which 3 were waited for; matrix products, arithmetic and copies ran while one was open for 3% of the time, Pallas kernels for 0%

profile of v1, /device:TPU:6, one launch (start us, length us, event | category | flops | bytes accessed | tf_op | source)
XLA Modules:
  0.0 488.7 jit_solution(17270684272276339798)
XLA Ops:
  8.0 2.7 collective-permute-start
  10.8 0.9 constant_dynamic-update-slice_fusion.1
  11.7 1.6 collective-permute-done
  13.5 1.3 collective-permute-start.1
  14.8 1.3 collective-permute-start.2
  16.1 1.1 copy.19
  17.4 2.7 collective-permute-done.2
  20.1 0.8 fusion.10
  24.0 0.9 copy.18
  24.9 3.6 reshape.65
  28.5 4.0 convolution_bitcast_fusion
  32.6 146.6 %all_gather.9 = bf16[384,2,4,160]{3,2,1,0:T(4,128)(2,1)S(1)} all-gather(bf16[24,2,4,160]{3,2,1,0:T(4,128)(2,1)S(1)} %copy-done.3), channel_id=1, replica_groups=mesh['tm'=4,'height'=8,'chan'=16] {'chan'}, dimensions={0}, use_global_device_ids=true | all-gather | bytes 1044480 | tf_op jit(solution)/shard_map/all_gather | solution.py:29
  179.2 1.4 copy.17
  180.7 0.4 multiply_reduce_fusion.1
  181.1 0.7 multiply_convert_fusion
  181.8 0.3 copy-done.1
  182.1 2.0 fusion.39
  184.1 1.0 copy.16
  185.5 277.7 %all-reduce.3.cloned.1.call-done = f32[384,1280]{0,1:T(8,128)} async-done(((f32[384,1280]{0,1:T(8,128)}), f32[384,1280]{0,1:T(8,128)}) %all-reduce.3.cloned.1.call-update) | async-done | bytes 1966096 | tf_op jit(solution)/shard_map/psum | solution.py:62
  463.1 3.0 multiply_reduce_fusion
  466.2 0.9 fusion.3
  467.1 0.9 copy.20
  467.9 11.6 %reduce_sum.29 = f32[648,384]{1,0:T(8,128)S(1)} reduce(f32[32,648,384]{2,1,0:T(8,128)} %bitcast.121, f32[]{:T(128)} %constant.10.clone.1), dimensions={0}, to_apply=%region_3.4 | reduce | flops 7713792 | bytes 32845828 | tf_op jit(solution)/shard_map/reduce_sum | solution.py:53
  479.7 1.5 copy.21
  (53 shorter events, 4.0 us)
Async XLA Ops:
  8.0 455.1 %all-reduce.3.cloned.1.call-start = ((), (), s32[]{:S(2)}) async-start(), calls=%async_computation | async-start | bytes 3932160 | tf_op jit(solution)/shard_map/psum | solution.py:62
  8.0 5.3 %collective-permute-start = (bf16[24,2,4,160]{3,2,1,0:T(4,128)(2,1)}, bf16[24,2,4,160]{3,2,1,0:T(4,128)(2,1)S(1)}, u32[]{:S(2)}, u32[]{:S(2)}) collective-permute-start(bf16[24,2,4,160]{3,2,1,0:T(4,128)(2,1)} %param.6), channel_id=1, source_target_pairs={{128,0},{256,128},{384,256},{129,1},{257,129},{385,257},{130,2},{2... | collective-permute-start | bytes 184328 | tf_op jit(solution)/shard_map/ppermute | solution.py:11
  13.5 3.9 collective-permute-start.1
  14.8 5.3 %collective-permute-start.2 = (bf16[24,4,1,160]{3,2,1,0:T(2,128)(2,1)S(1)}, bf16[24,4,1,160]{3,2,1,0:T(2,128)(2,1)S(1)}, u32[]{:S(2)}, u32[]{:S(2)}) collective-permute-start(bf16[24,4,1,160]{3,2,1,0:T(2,128)(2,1)S(1)} %get-tuple-element.11), channel_id=1, source_target_pairs={{16,0},{32,16},{48,32},{64,48},{80,64},{96,80},{112,96},{17,1},{33... | collective-permute-start | bytes 92168 | tf_op jit(solution)/shard_map/ppermute | solution.py:22
  20.9 2.6 copy-start.2
  28.5 4.1 copy-start.3
  32.5 148.6 %copy-start.4 = (f32[384]{0:T(512)S(1)}, f32[384]{0:T(512)}, u32[]{:S(2)}) copy-start(f32[384]{0:T(512)} %param.9) | copy-start | bytes 4612
  32.5 148.6 %copy-start.5 = (f32[384]{0:T(512)S(1)}, f32[384]{0:T(512)}, u32[]{:S(2)}) copy-start(f32[384]{0:T(512)} %param.8) | copy-start | bytes 4612
  32.5 435.4 %all-gather.3.cloned.1.call-start = ((), (), s32[]{:S(2)}) async-start(), calls=%async_computation.1 | async-start | bytes 32845824 | tf_op jit(solution)/shard_map/all_gather | solution.py:53
  180.6 1.4 copy-start.1
  463.1 3.0 copy-start
Sparse Core Ops, SparseCore 0:
  32.6 430.4 all-reduce.2
Sparse Core Ops, SparseCore 1:
  184.2 251.7 all-gather.2

commit v2 on v0

--- a/solution.py
+++ b/solution.py
@@ -26,7 +26,9 @@
 
 def on_device(features, cotangent, conv_weight, norm_gain, norm_bias):
     chans, frames, rows, cols = features.shape
-    whole_x = lax.all_gather(features, "chan", axis=0, tiled=True)
+    whole_x = jnp.concatenate(
+        lax.all_to_all(jnp.stack([features] * lax.axis_size("chan")), "chan", 0, 0), axis=0
+    )
     total = whole_x.shape[0]
     flat_x = whole_x.reshape(total, -1).astype(jnp.float32)
     inv_rms = lax.rsqrt(jnp.mean(flat_x * flat_x, axis=0, keepdims=True) + 1e-06)

time: 688 us -> 642 us (0.933)
  the two profiles are of different devices: /device:TPU:6 before, /device:TPU:8 now
where the time goes in v2:
time: 642 us
  waiting for transfers between devices  562 us (88%)
  local copies, waits for them, and re-layouts  25.5 us (4%)
  starting transfers between devices  22.5 us (4%)
  between operations  14.3 us (2%)
  other arithmetic  9.97 us (2%)
  matrix products  7.32 us (1%)
    psum x1, waiting for transfers between devices, on_device(): summed = lax.psum(local_sums, ('tm', 'height'))  289 us
    psum x1, waiting for transfers between devices, on_device(): act_grad = lax.psum(partial_value, 'chan')  250 us
    all_to_all x1, waiting for transfers between devices, on_device(): lax.all_to_all(jnp.stack([features] * lax.axis_size('chan')), 'chan', 0, 0)  18.7 us
    all_to_all x1, starting transfers between devices, on_device(): lax.all_to_all(jnp.stack([features] * lax.axis_size('chan')), 'chan', 0, 0)  18.2 us
  transfers between devices with their start and end apart: 6, of which 4 were waited for; matrix products, arithmetic and copies ran while one was open for 6% of the time, Pallas kernels for 0%

profile of v2, /device:TPU:8, one launch (start us, length us, event | category | flops | bytes accessed | tf_op | source)
XLA Modules:
  0.0 641.9 jit_solution(17059971808967866668)
XLA Ops:
  7.2 1.3 collective-permute-start
  8.5 0.9 constant_dynamic-update-slice_fusion.1
  9.4 4.5 collective-permute-done
  14.1 1.3 collective-permute-start.1
  15.4 1.4 collective-permute-start.2
  16.9 2.7 stack.103
  19.5 18.2 %all-to-all-start = ((bf16[16,24,2,4,160]{4,3,2,1,0:T(4,128)(2,1)}), bf16[16,24,2,4,160]{4,3,2,1,0:T(4,128)(2,1)S(1)}, u32[]{:S(2)}, u32[]{:S(2)}) async-start(bf16[16,24,2,4,160]{4,3,2,1,0:T(4,128)(2,1)} %stack.103), calls=%async_computation | async-start | bytes 3145728 | tf_op jit(solution)/shard_map/all_to_all | solution.py:30
  37.8 1.1 copy.11
  39.1 1.0 reshape.66
  43.9 2.4 copy.12
  46.4 5.5 reshape.65
  51.9 3.9 convolution_bitcast_fusion
  56.0 18.7 %all-to-all-done = bf16[16,24,2,4,160]{4,3,2,1,0:T(4,128)(2,1)S(1)} async-done(((bf16[16,24,2,4,160]{4,3,2,1,0:T(4,128)(2,1)}), bf16[16,24,2,4,160]{4,3,2,1,0:T(4,128)(2,1)S(1)}, u32[]{:S(2)}, u32[]{:S(2)}) %all-to-all-start) | async-done | bytes 983072 | tf_op jit(solution)/shard_map/all_to_all | solution.py:30
  74.8 1.0 multiply_reduce_fusion
  75.8 2.3 fusion
  78.2 2.4 convert_element_type.34
  80.5 2.5 reshape.70
  83.0 2.0 copy.14
  85.0 3.4 fusion.40
  88.5 249.6 %all-reduce.4.cloned.1.call-done = f32[384,1280]{0,1:T(8,128)} async-done(((f32[384,1280]{0,1:T(8,128)}), f32[384,1280]{0,1:T(8,128)}) %all-reduce.4.cloned.1.call-update) | async-done | bytes 1966096 | tf_op jit(solution)/shard_map/psum | solution.py:64
  338.1 2.8 multiply_reduce_fusion.1
  342.6 289.5 %all-reduce.6.cloned.1.call-done = f32[648,384]{1,0:T(8,128)} async-done(((f32[648,384]{1,0:T(8,128)}), f32[648,384]{1,0:T(8,128)}) %all-reduce.6.cloned.1.call-update) | async-done | bytes 995344 | tf_op jit(solution)/shard_map/psum | solution.py:55
  632.1 1.3 broadcast_multiply_fusion
  633.6 1.5 copy.18
  (59 shorter events, 6.5 us)
Async XLA Ops:
  7.2 6.7 %collective-permute-start = (bf16[24,2,4,160]{3,2,1,0:T(4,128)(2,1)}, bf16[24,2,4,160]{3,2,1,0:T(4,128)(2,1)S(1)}, u32[]{:S(2)}, u32[]{:S(2)}) collective-permute-start(bf16[24,2,4,160]{3,2,1,0:T(4,128)(2,1)} %param.6), channel_id=1, source_target_pairs={{128,0},{256,128},{384,256},{129,1},{257,129},{385,257},{130,2},{2... | collective-permute-start | bytes 184328 | tf_op jit(solution)/shard_map/ppermute | solution.py:11
  13.9 23.8 %copy-start.3 = (bf16[24,2,4,160]{3,2,1,0:T(4,128)(2,1)S(1)}, bf16[24,2,4,160]{3,2,1,0:T(4,128)(2,1)}, u32[]{:S(2)}) copy-start(bf16[24,2,4,160]{3,2,1,0:T(4,128)(2,1)} %param.6) | copy-start | bytes 184324
  14.1 26.0 %collective-permute-start.1 = (bf16[24,4,1,160]{3,2,1,0:T(2,128)(2,1)S(1)}, bf16[24,4,1,160]{3,2,1,0:T(2,128)(2,1)S(1)}, u32[]{:S(2)}, u32[]{:S(2)}) collective-permute-start(bf16[24,4,1,160]{3,2,1,0:T(2,128)(2,1)S(1)} %get-tuple-element.8), channel_id=1, source_target_pairs={{0,16},{16,32},{32,48},{48,64},{64,80},{80,96},{96,112},{1,17},{17... | collective-permute-start | bytes 92168 | tf_op jit(solution)/shard_map/ppermute | solution.py:21
  15.4 23.4 %copy-start.5 = (f32[384]{0:T(512)S(1)}, f32[384]{0:T(512)}, u32[]{:S(2)}) copy-start(f32[384]{0:T(512)} %param.9) | copy-start | bytes 4612
  15.4 23.5 %copy-start.6 = (f32[384]{0:T(512)S(1)}, f32[384]{0:T(512)}, u32[]{:S(2)}) copy-start(f32[384]{0:T(512)} %param.8) | copy-start | bytes 4612
  15.4 23.6 %copy-start.4 = (bf16[24,27,384]{2,0,1:T(8,128)(2,1)S(1)}, bf16[24,27,384]{2,0,1:T(8,128)(2,1)}, u32[]{:S(2)}) copy-start(bf16[24,27,384]{2,0,1:T(8,128)(2,1)} %param.7) | copy-start | bytes 1492996
  15.4 24.7 %collective-permute-start.2 = (bf16[24,4,1,160]{3,2,1,0:T(2,128)(2,1)S(1)}, bf16[24,4,1,160]{3,2,1,0:T(2,128)(2,1)S(1)}, u32[]{:S(2)}, u32[]{:S(2)}) collective-permute-start(bf16[24,4,1,160]{3,2,1,0:T(2,128)(2,1)S(1)} %get-tuple-element.9), channel_id=1, source_target_pairs={{16,0},{32,16},{48,32},{64,48},{80,64},{96,80},{112,96},{17,1},{33... | collective-permute-start | bytes 92168 | tf_op jit(solution)/shard_map/ppermute | solution.py:22
  19.5 55.2 %all-to-all-start = ((bf16[16,24,2,4,160]{4,3,2,1,0:T(4,128)(2,1)}), bf16[16,24,2,4,160]{4,3,2,1,0:T(4,128)(2,1)S(1)}, u32[]{:S(2)}, u32[]{:S(2)}) async-start(bf16[16,24,2,4,160]{4,3,2,1,0:T(4,128)(2,1)} %stack.103), calls=%async_computation | async-start | bytes 3145728 | tf_op jit(solution)/shard_map/all_to_all | solution.py:30
  37.7 300.3 %all-reduce.4.cloned.1.call-start = ((), (), s32[]{:S(2)}) async-start(), calls=%async_computation.1 | async-start | bytes 3932160 | tf_op jit(solution)/shard_map/psum | solution.py:64
  51.9 3.9 copy-start.1
  55.8 576.3 %all-reduce.6.cloned.1.call-start = ((), (), s32[]{:S(2)}) async-start(), calls=%async_computation.2 | async-start | bytes 1990656 | tf_op jit(solution)/shard_map/psum | solution.py:55
  83.0 2.0 copy-start.2
  88.5 252.4 %copy-start = (f32[24,2,4,160]{0,3,2,1:T(8,128)S(1)}, f32[24,2,4,160]{0,3,2,1:T(8,128)}, u32[]{:S(2)}) copy-start(f32[24,2,4,160]{0,3,2,1:T(8,128)} %copy.11) | copy-start | bytes 368644
Sparse Core Ops, SparseCore 0:
  55.9 282.1 all-reduce.3
  341.8 290.2 all-reduce.5

commit v3 on v0

--- a/solution.py
+++ b/solution.py
@@ -50,7 +50,7 @@
         stacked, active, (((1,), (1,)), ((), ())), preferred_element_type=jnp.float32
     )
     positions = frames * lax.axis_size("tm") * rows * lax.axis_size("height") * cols
-    summed = lax.psum(local_sums, ("tm", "height"))
+    summed = lax.psum(lax.psum(local_sums, "height"), "tm")
     weight_grad = (summed / math.sqrt(positions)).reshape(chans, 27, total)
     sig = jax.nn.sigmoid(normed)
     slope = sig * (1.0 + normed * (1.0 - sig))

time: 688 us -> 539 us (0.78)
  waiting for transfers between devices: 534 us -> 387 us
    psum x1 -> x2, waiting for transfers between devices: 262 us -> 128 us  [on_device(): summed = lax.psum(lax.psum(local_sums, 'height'), 'tm')]
    psum x1, waiting for transfers between devices: 273 us -> 259 us  [on_device(): act_grad = lax.psum(partial_value, 'chan')]
  transfers between devices with their start and end apart: 5 -> 6, of which waited for: 3 -> 4; matrix products, arithmetic and copies ran while one was open for 2% -> 3% of each run, Pallas kernels for 0% -> 0%
where the time goes in v3:
time: 539 us; the launch traced here: 537 us
  waiting for transfers between devices  387 us (72%)
  blocking collectives  96.6 us (18%)
  local copies, waits for them, and re-layouts  17.4 us (3%)
  between operations  14 us (3%)
  other arithmetic  9.18 us (2%)
  matrix products  6.73 us (1%)
  starting transfers between devices  6.2 us (1%)
    psum x1, waiting for transfers between devices, on_device(): act_grad = lax.psum(partial_value, 'chan')  259 us
    psum x2, waiting for transfers between devices, on_device(): summed = lax.psum(lax.psum(local_sums, 'height'), 'tm')  128 us
    all_gather x1, blocking collectives, on_device(): whole_x = lax.all_gather(features, 'chan', axis=0, tiled=True)  96.6 us
  transfers between devices with their start and end apart: 6, of which 4 were waited for; matrix products, arithmetic and copies ran while one was open for 3% of the time, Pallas kernels for 0%

profile of v3, /device:TPU:6, one launch (start us, length us, event | category | flops | bytes accessed | tf_op | source)
XLA Modules:
  0.0 537.0 jit_solution(4207273386043271604)
XLA Ops:
  7.2 2.7 collective-permute-start
  10.0 96.6 %all_gather.3 = bf16[384,2,4,160]{3,2,1,0:T(4,128)(2,1)S(1)} all-gather(bf16[24,2,4,160]{3,2,1,0:T(4,128)(2,1)} %param.5), channel_id=1, replica_groups=mesh['tm'=4,'height'=8,'chan'=16] {'chan'}, dimensions={0}, use_global_device_ids=true | all-gather | bytes 1044480 | tf_op jit(solution)/shard_map/all_gather | solution.py:29
  106.5 1.4 copy.18
  108.0 0.4 multiply_reduce_fusion.1
  108.6 1.9 collective-permute-start.1
  110.5 1.3 collective-permute-start.2
  111.8 1.7 multiply_convert_fusion
  113.7 0.8 fusion.10
  117.6 2.4 copy.19
  120.0 5.5 %reshape.64 = bf16[648,1280]{1,0:T(8,128)(2,1)S(1)} reshape(bf16[24,27,2,4,160]{4,3,2,1,0:T(4,128)(2,1)} %copy.19) | data formatting | bytes 3317760 | tf_op jit(solution)/shard_map/reshape | solution.py:48
  125.5 3.2 fusion.39
  128.7 1.1 copy.20
  129.8 1.0 reshape.65
  130.8 3.6 convolution_bitcast_fusion
  134.7 1.0 copy.17
  135.7 0.2 bitcast_convert_fusion
  136.0 75.6 %all-reduce.7.cloned.1.call-done = f32[648,384]{1,0:T(8,128)} async-done(((f32[648,384]{1,0:T(8,128)}), f32[648,384]{1,0:T(8,128)}) %all-reduce.7.cloned.1.call-update) | async-done | bytes 995344 | tf_op jit(solution)/shard_map/psum | solution.py:53
  211.6 259.1 %all-reduce.5.cloned.1.call-done = f32[384,1280]{0,1:T(8,128)} async-done(((f32[384,1280]{0,1:T(8,128)}), f32[384,1280]{0,1:T(8,128)}) %all-reduce.5.cloned.1.call-update) | async-done | bytes 1966096 | tf_op jit(solution)/shard_map/psum | solution.py:62
  470.6 3.0 multiply_reduce_fusion
  473.7 0.9 fusion.3
  474.6 0.8 copy.21
  475.5 52.1 %all-reduce.9.cloned.1.call-done = f32[648,384]{1,0:T(8,128)} async-done(((f32[648,384]{1,0:T(8,128)}), f32[648,384]{1,0:T(8,128)}) %all-reduce.9.cloned.1.call-update) | async-done | bytes 995344 | tf_op jit(solution)/shard_map/psum | solution.py:53
  527.6 1.3 broadcast_multiply_fusion
  529.0 1.5 copy.22
  (51 shorter events, 4.0 us)
Async XLA Ops:
  7.2 101.2 %copy-start.1 = (bf16[24,2,4,160]{3,2,1,0:T(4,128)(2,1)S(1)}, bf16[24,2,4,160]{3,2,1,0:T(4,128)(2,1)}, u32[]{:S(2)}) copy-start(bf16[24,2,4,160]{3,2,1,0:T(4,128)(2,1)} %param.6) | copy-start | bytes 184324
  7.2 104.6 %copy-start.3 = (f32[384]{0:T(512)S(1)}, f32[384]{0:T(512)}, u32[]{:S(2)}) copy-start(f32[384]{0:T(512)} %param.8) | copy-start | bytes 4612
  7.2 104.6 %copy-start.2 = (f32[384]{0:T(512)S(1)}, f32[384]{0:T(512)}, u32[]{:S(2)}) copy-start(f32[384]{0:T(512)} %param.9) | copy-start | bytes 4612
  7.2 204.3 %all-reduce.7.cloned.1.call-start = ((), (), s32[]{:S(2)}) async-start(), calls=%async_computation.1 | async-start | bytes 1990656 | tf_op jit(solution)/shard_map/psum | solution.py:53
  7.2 101.2 %collective-permute-start = (bf16[24,2,4,160]{3,2,1,0:T(4,128)(2,1)}, bf16[24,2,4,160]{3,2,1,0:T(4,128)(2,1)S(1)}, u32[]{:S(2)}, u32[]{:S(2)}) collective-permute-start(bf16[24,2,4,160]{3,2,1,0:T(4,128)(2,1)} %param.6), channel_id=1, source_target_pairs={{128,0},{256,128},{384,256},{129,1},{257,129},{385,257},{130,2},{2... | collective-permute-start | bytes 184328 | tf_op jit(solution)/shard_map/ppermute | solution.py:11
  108.6 4.9 collective-permute-start.1
  110.5 3.2 collective-permute-start.2
  128.7 342.0 %all-reduce.5.cloned.1.call-start = ((), (), s32[]{:S(2)}) async-start(), calls=%async_computation | async-start | bytes 3932160 | tf_op jit(solution)/shard_map/psum | solution.py:62
  134.4 393.2 %all-reduce.9.cloned.1.call-start = ((), (), s32[]{:S(2)}) async-start(), calls=%async_computation.2 | async-start | bytes 1990656 | tf_op jit(solution)/shard_map/psum | solution.py:53
  470.6 3.0 copy-start
Sparse Core Ops, SparseCore 0:
  128.8 82.6 all-reduce.6
  214.5 256.1 all-reduce.4
  473.2 54.3 all-reduce.8
